TPU v7x, 512 devices: a whole 4x8x8 slice. The times are simulated.
512 devices in a mesh: side: 2 (over y_hi), vocab: 128 (over y_lo, x, z), tok: 2 (over core).
Axes of the slice: x: 4, y: 8 (y_hi: 2, y_lo: 4; y = y_hi * 4 + y_lo), z: 8, core: 2. Of those that a mesh axis runs over, the one named last changes fastest.
Arguments:
- reward_hidden: bfloat16 [2, 320, 2048], P('side', None, 'tok'), may hold values from -66 to 66
- reward_heads: bfloat16 [2, 2048, 151936], P('side', 'tok', 'vocab'), may hold values from -6 to 6
- policy_hidden: bfloat16 [320, 2048], P(None, ('side', 'tok')), may hold values from -66 to 66
- policy_head: bfloat16 [2048, 151936], P(('side', 'tok'), 'vocab'), may hold values from -6 to 6
- targets: int32 [320], replicated, may hold values from 0 to 151935
- response_mask: int32 [320], replicated, may hold values 0 or 1
- rollout_ids: int32 [320], replicated, may hold values from 0 to 3, never falling along the last dimension, each value on 1 to 160 neighbouring positions
Outputs:
- rewards: float32 [320], replicated
- hidden_grad: bfloat16 [320, 2048], P(None, ('side', 'tok'))
All inputs are finite; a program needn't handle non-finite values.
Results may differ from a plain program's by a relative error of at most 0.005.
Values may be sent and summed in bfloat16 or wider, within the bound.
A program may use at most 64 MiB of HBM per device.

v0:
```python
import jax
import jax.numpy as jnp
from jax import lax
from jax.sharding import PartitionSpec as P

BETA = 0.05


def pick_target(logits, wanted, first_column):
    columns = first_column + lax.broadcasted_iota(jnp.int32, logits.shape, 1)
    return jnp.sum(jnp.where(columns == wanted[:, None], logits, 0.0), axis=1)


def per_device(
    reward_hidden, reward_heads, policy_hidden, policy_head, targets, response_mask, rollout_ids
):
    features = reward_hidden[0]
    head_slab = reward_heads[0]
    window = features.shape[0]
    slab_width = head_slab.shape[1]
    block_rows = window // lax.axis_size("tok")
    first_column = lax.axis_index("vocab") * slab_width
    block_start = lax.axis_index("tok") * block_rows
    reward_logits = lax.psum_scatter(
        jnp.dot(features, head_slab, preferred_element_type=jnp.float32),
        "tok",
        scatter_dimension=0,
        tiled=True,
    )
    reward_targets = lax.dynamic_slice_in_dim(targets, block_start, block_rows, 0)
    reward_pick = pick_target(reward_logits, reward_targets, first_column)
    reward_top = jnp.max(reward_logits, axis=1)
    policy_part = jnp.dot(policy_hidden, policy_head, preferred_element_type=jnp.float32)
    policy_logits = lax.psum(policy_part, ("side", "tok"))
    policy_top = jnp.max(policy_logits, axis=1)
    reward_top, policy_top = lax.pmax((reward_top, policy_top), "vocab")
    reward_total = jnp.sum(jnp.exp(reward_logits - reward_top[:, None]), axis=1)
    policy_exp = jnp.exp(policy_logits - policy_top[:, None])
    policy_total = jnp.sum(policy_exp, axis=1)
    reward_total, reward_pick, policy_total = lax.psum(
        (reward_total, reward_pick, policy_total), "vocab"
    )
    policy_probs = policy_exp / policy_total[:, None]
    reward_logp = reward_pick - reward_top - jnp.log(reward_total)
    logprob_pairs = lax.all_gather(
        reward_logp[None, :], ("side", "tok"), axis=0, tiled=True
    ).reshape(2, window)
    live_tokens = response_mask.astype(jnp.float32)
    rewards = BETA * live_tokens * (logprob_pairs[0] - logprob_pairs[1])
    row_index = lax.broadcasted_iota(jnp.int32, (window, window), 0)
    column_index = lax.broadcasted_iota(jnp.int32, (window, window), 1)
    same_rollout = (rollout_ids[:, None] == rollout_ids[None, :]) & (column_index >= row_index)
    returns = jnp.sum(jnp.where(same_rollout, rewards[None, :], 0.0), axis=1)
    token_weight = live_tokens * returns
    columns = first_column + lax.broadcasted_iota(jnp.int32, policy_probs.shape, 1)
    onehot = (columns == targets[:, None]).astype(jnp.float32)
    logit_grad = (token_weight[:, None] * (policy_probs - onehot)).astype(jnp.bfloat16)
    partial_grad = lax.dot_general(
        logit_grad, policy_head, (((1,), (1,)), ((), ())), preferred_element_type=jnp.float32
    )
    hidden_grad = lax.psum(partial_grad, "vocab").astype(jnp.bfloat16)
    return (rewards, hidden_grad)


def solution(mesh):
    placed = (
        P("side", None, "tok"),
        P("side", "tok", "vocab"),
        P(None, ("side", "tok")),
        P(("side", "tok"), "vocab"),
        P(),
        P(),
        P(),
    )
    return jax.shard_map(
        per_device,
        mesh=mesh,
        in_specs=placed,
        out_specs=(P(), P(None, ("side", "tok"))),
        check_vma=False,
    )
```

profile of v0, /device:TPU:32, one launch (start us, length us, event | category | flops | bytes accessed | tf_op | source)
XLA Modules:
  0.0 1583.3 jit_solution(17041308352664230246)
XLA Ops:
  8.0 0.0 copy-start
  8.0 0.0 copy-start.6
  8.0 0.0 all-reduce.6.cloned.1.call-start
  8.1 3.3 fusion.6
  11.4 0.0 all-reduce.6.cloned.1.call-update
  11.4 0.0 reduce-scatter.2.cloned.1.call-start
  11.5 0.0 copy-done
  11.5 0.0 copy-done.6
  11.5 2.2 fusion
  13.7 0.0 copy-start.5
  13.7 0.0 reduce-scatter.2.cloned.1.call-update
  13.8 0.6 copy-done.5
  14.4 0.1 dynamic_slice.3
  14.5 1.3 dynamic-slice
  16.4 88.2 %all-reduce.6.cloned.1.call-done = f32[320,1187]{1,0:T(8,128)} async-done(((f32[320,1187]{1,0:T(8,128)}), f32[320,1187]{1,0:T(8,128)}) %all-reduce.6.cloned.1.call-update) | async-done | bytes 1519376 | tf_op jit(solution)/shard_map/psum | solution.py:34
  104.6 1.6 reduce_max.19
  106.2 0.0 copy-start.3
  106.2 0.0 copy-start.2
  106.2 0.0 reduce-scatter.2.cloned.1.call-done
  106.2 0.0 copy-start.1
  106.2 1.3 reduce_max.18
  107.6 365.2 %all-reduce.2 = (f32[160]{0:T(256)S(1)}, f32[320]{0:T(512)S(1)}) all-reduce(f32[160]{0:T(256)S(1)} %reduce_max.18, f32[320]{0:T(512)S(1)} %reduce_max.19), channel_id=1, replica_groups=mesh['side'=2,'vocab'=128,'tok'=2] {'vocab'}, use_global_device_ids=true, to_apply=%region_4.5 | all-reduce | flops 480 | bytes 3840 | tf_op jit(solution)/shard_map/pmax | solution.py:36
  472.8 1.8 fusion.2
  474.6 0.0 copy-done.1
  474.6 0.4 select_reduce_fusion
  475.0 360.9 %all-reduce.1 = (f32[160]{0:T(256)S(1)}, f32[160]{0:T(256)S(1)}, f32[320]{0:T(512)S(1)}) all-reduce(f32[160]{0:T(256)S(1)} %get-tuple-element.3, f32[160]{0:T(256)S(1)} %get-tuple-element.2, f32[320]{0:T(512)S(1)} %fusion.2), channel_id=1, replica_groups=mesh['side'=2,'vocab'=128,'tok'=2] {'vocab'}, use_global_device_ids=true, to_apply=%region_6.7 | all-reduce | flops 640 | bytes 5120 | tf_op jit(solution)/shard_map/psum | solution.py:40
  835.9 0.1 subtract_dynamic-update-slice_fusion
  836.0 9.6 all-reduce
  845.6 0.0 copy-done.3
  845.6 0.1 subtract_multiply_fusion
  845.6 0.0 copy-done.2
  845.6 0.0 copy-start.4
  845.6 0.2 select_reduce_fusion.1
  845.9 2.5 fusion.3
  848.4 0.0 copy-done.4
  848.4 727.4 %all-reduce.7 = bf16[320,512]{1,0:T(8,128)(2,1)} all-reduce(f32[320,512]{1,0:T(8,128)S(1)} %fusion.3), channel_id=1, replica_groups=mesh['side'=2,'vocab'=128,'tok'=2] {'vocab'}, use_global_device_ids=true, to_apply=%region_13.14 | all-reduce | flops 163840 | bytes 983040 | tf_op jit(solution)/shard_map/psum | solution.py:61
  (3 shorter events, 0.0 us)
Async XLA Ops:
  8.0 3.5 copy-start
  8.0 3.5 copy-start.6
  8.0 96.6 %all-reduce.6.cloned.1.call-start = ((), (), s32[]{:S(2)}) async-start(), calls=%async_computation.2 | async-start | bytes 3276800 | tf_op jit(solution)/shard_map/psum | solution.py:34
  11.4 94.8 %reduce-scatter.2.cloned.1.call-start = ((), (), s32[]{:S(2)}) async-start(), calls=%async_computation.1 | async-start | bytes 2457600 | tf_op jit(solution)/shard_map/reduce_scatter | solution.py:24
  13.7 0.7 copy-start.5
  106.2 739.4 %copy-start.3 = (s32[320]{0:T(512)S(1)}, s32[320]{0:T(512)}, u32[]{:S(2)}) copy-start(s32[320]{0:T(512)} %param.12) | copy-start | bytes 3844
  106.2 739.5 %copy-start.2 = (s32[320]{0:T(512)S(1)}, s32[320]{0:T(512)}, u32[]{:S(2)}) copy-start(s32[320]{0:T(512)} %param.13) | copy-start | bytes 3844
  106.2 368.4 %copy-start.1 = (f32[160,1187]{1,0:T(8,128)S(1)}, f32[160,1187]{1,0:T(8,128)}, u32[]{:S(2)}) copy-start(f32[160,1187]{1,0:T(8,128)} %reduce-scatter.2.cloned.1.call-done) | copy-start | bytes 2279044
  845.6 2.8 copy-start.4
Sparse Core Ops, SparseCore 0:
  12.1 92.4 all-reduce.5
Sparse Core Ops, SparseCore 1:
  14.7 21.5 reduce-scatter.1
where the time goes:
time: 1580 us
  blocking collectives  1460 us (92%)
  waiting for transfers between devices  88.2 us (6%)
  between operations  16.2 us (1%)
    psum x1, blocking collectives, per_device(): hidden_grad = lax.psum(partial_grad, 'vocab').astype(jnp.bfloat16)  727 us
    pmax x1, blocking collectives, per_device(): reward_top, policy_top = lax.pmax((reward_top, policy_top), 'vocab')  365 us
    psum x1, blocking collectives, per_device(): lax.psum((reward_total, reward_pick, policy_total), 'vocab')  361 us
    psum x1, waiting for transfers between devices, per_device(): policy_logits = lax.psum(policy_part, ('side', 'tok'))  88.2 us
  transfers between devices with their start and end apart: 2, of which 1 were waited for; matrix products, arithmetic and copies ran while one was open for 0% of the time, Pallas kernels for 0%

commit v1 on v0

v1 whole, which is shorter than its diff:
```python
import functools
import math

import jax
import jax.numpy as jnp
from jax import lax
from jax.experimental import pallas as pl
from jax.experimental.pallas import tpu as pltpu
from jax.sharding import PartitionSpec as P

BETA = 0.05
MESH = pl.DeviceIdType.MESH
F32 = jnp.float32
NX, NYL, NZ = 4, 4, 8
NY = 2 * NYL
W = 320
HALF = 160
RC = 32
NCH = HALF // RC
CR = 2 * RC
ZR = CR // NZ
LANES = 128
STEP = math.log(2.0) / 16.0
FULL = 32700.0
LOW = -1e30
NSEM = 256


def nt_dot(a, b):
    return lax.dot_general(a, b, (((1,), (1,)), ((), ())), preferred_element_type=F32)


def kernel(
    v,
    rh_hbm, rw_hbm, ph_hbm, pw_hbm, colinfo, rowinfo,
    rew, hg,
    rh, rw, ph, pw, pp, pr, qs, qr, eb, st,
    rp, rr, gs, xr, zs, zr, yr, zag, hx,
    hs, hxr, hz, hzr, hfin, rz, rx, ry, rc, wv,
    load_sem, send_sem, recv_sem,
):
    vp = pp.shape[1]
    feats = ph.shape[1]
    side = lax.axis_index("side")
    vocab = lax.axis_index("vocab")
    tok = lax.axis_index("tok")
    ylo = lax.div(vocab, NX * NZ)
    x = lax.rem(lax.div(vocab, NZ), NX)
    z = lax.rem(vocab, NZ)
    y = side * NYL + ylo
    first = vocab * v

    def at(yy, xx, zz, tt):
        return (lax.div(yy, NYL), lax.rem(yy, NYL) * (NX * NZ) + xx * NZ + zz, tt)

    core_peer = at(y, x, z, 1 - tok)
    side_peer = at(lax.rem(y + NYL, NY), x, z, tok)
    xs = [lax.rem(x + d, NX) for d in range(NX)]
    zs_ = [lax.rem(z + d, NZ) for d in range(NZ)]
    x_peer = [at(y, xs[d], z, tok) for d in range(NX)]
    z_peer = [at(y, x, zs_[d], tok) for d in range(NZ)]
    y_peer = [at(lax.rem(y + d, NY), x, z, tok) for d in range(NY)]
    yls = [lax.rem(ylo + d, NYL) for d in range(NYL)]
    yl_peer = [at(side * NYL + yls[d], x, z, tok) for d in range(NYL)]

    loads = [
        pltpu.make_async_copy(ph_hbm, ph, load_sem.at[0]),
        pltpu.make_async_copy(pw_hbm, pw, load_sem.at[1]),
        pltpu.make_async_copy(rh_hbm.at[0], rh, load_sem.at[2]),
        pltpu.make_async_copy(rw_hbm.at[0], rw, load_sem.at[3]),
    ]
    for c in loads:
        c.start()

    barrier = pltpu.get_barrier_semaphore()
    peers = [core_peer] + x_peer[1:] + z_peer[1:] + y_peer[1:]
    for p in peers:
        pl.semaphore_signal(barrier, inc=1, device_id=p, device_id_type=MESH)

    copies = []

    def send(src, dst, peer):
        i = len(copies)
        c = pltpu.make_async_remote_copy(
            src_ref=src, dst_ref=dst, send_sem=send_sem.at[i], recv_sem=recv_sem.at[i],
            device_id=peer, device_id_type=MESH,
        )
        c.start()
        copies.append(c)
        return c

    def landed(group):
        for c in group:
            c.wait_recv()

    tail = vp - LANES
    for buf in (pp, rp):
        buf[:, tail:] = jnp.zeros((W, LANES), F32)
    eb[:, tail:] = jnp.zeros((W, LANES), eb.dtype)

    own = pl.multiple_of(tok * HALF, HALF)
    other = pl.multiple_of((1 - tok) * HALF, HALF)

    loads[0].wait()
    loads[1].wait()
    pp[pl.ds(other, HALF), :v] = jnp.dot(ph[pl.ds(other, HALF), :], pw[...], preferred_element_type=F32)
    pl.semaphore_wait(barrier, len(peers))
    core_p = []
    for c in range(NCH):
        core_p.append(send(pp.at[pl.ds(other + RC * c, RC), :], pr.at[pl.ds(RC * c, RC), :], core_peer))
    pp[pl.ds(own, HALF), :v] = jnp.dot(ph[pl.ds(own, HALF), :], pw[...], preferred_element_type=F32)

    lane = lax.broadcasted_iota(jnp.int32, (RC, vp), 1)
    st_lane = lax.broadcasted_iota(jnp.int32, (RC, LANES), 1)

    side_p = []
    for c in range(NCH):
        landed([core_p[c]])
        rows = pl.ds(pl.multiple_of(own + RC * c, RC), RC)
        part = pp[rows, :] + pr[pl.ds(RC * c, RC), :]
        pp[rows, :] = part
        top = jnp.maximum(jnp.max(jnp.abs(part), axis=1, keepdims=True), 1e-6)
        expo = jnp.ceil(jnp.log(top) / STEP)
        inv = FULL * jnp.exp(expo * -STEP)
        quant = jnp.clip(jnp.round(part * inv), -32767.0, 32767.0)
        quant = jnp.where(lane == vp - 1, expo, quant)
        qs[pl.ds(RC * c, RC), :] = quant.astype(jnp.int32).astype(jnp.int16)
        side_p.append(send(qs.at[pl.ds(RC * c, RC), :], qr.at[pl.ds(RC * c, RC), :], side_peer))

    wide = lax.broadcasted_iota(jnp.int32, (W, v), 1) + first
    hot = (wide == colinfo[:, 0:1]).astype(jnp.bfloat16)
    picked = nt_dot(hot, pw[...]).astype(jnp.bfloat16)
    for i in range(NX):
        hs[i] = picked[:, LANES * i:LANES * (i + 1)]
    h_x = [send(hs.at[xs[d]], hxr.at[d - 1], x_peer[d]) for d in range(1, NX)]

    loads[2].wait()
    loads[3].wait()
    rp[pl.ds(other, HALF), :v] = jnp.dot(rh[pl.ds(other, HALF), :], rw[...], preferred_element_type=F32)
    core_r = send(rp.at[pl.ds(other, HALF), :], rr, core_peer)
    rp[pl.ds(own, HALF), :v] = jnp.dot(rh[pl.ds(own, HALF), :], rw[...], preferred_element_type=F32)
    landed([core_r])
    stats = []
    for c in range(NCH):
        rows = pl.ds(pl.multiple_of(own + RC * c, RC), RC)
        logit = rp[rows, :] + rr[pl.ds(RC * c, RC), :]
        logit = jnp.where(lane < v, logit, LOW)
        m = jnp.max(logit, axis=1, keepdims=True)
        s = jnp.sum(jnp.exp(logit - m), axis=1, keepdims=True)
        is_target = (lane + first == colinfo[rows, 0:1]) & (lane < v)
        pick = jnp.sum(jnp.where(is_target, logit, 0.0), axis=1, keepdims=True)
        stats.append(jnp.where(st_lane == 0, m, jnp.where(st_lane == 1, s, jnp.where(st_lane == 2, pick, 0.0))))
    stats.append(jnp.zeros((256 - HALF, LANES), F32))
    rz[z] = jnp.transpose(jnp.concatenate(stats, axis=0))[:8, :]
    r_z = [send(rz.at[z], rz.at[z], z_peer[d]) for d in range(1, NZ)]

    def merge_rows(buf, lo, hi):
        tiles = [buf[i] for i in range(lo, hi)]
        m = tiles[0][0:1]
        for t in tiles[1:]:
            m = jnp.maximum(m, t[0:1])
        s = jnp.zeros_like(m)
        pick = jnp.zeros_like(m)
        for t in tiles:
            s = s + jnp.exp(t[0:1] - m) * t[1:2]
            pick = pick + t[2:3]
        return m, s, pick

    def pack_rows(m, s, pick):
        row = lax.broadcasted_iota(jnp.int32, (8, 256), 0)
        return jnp.where(row == 0, m, jnp.where(row == 1, s, jnp.where(row == 2, pick, 0.0)))

    landed(h_x)
    h_own = hs[x].astype(F32)
    for d in range(1, NX):
        h_own = h_own + hxr[d - 1].astype(F32)
    hz[...] = h_own.reshape(2, NCH, RC, LANES)
    per_blk = RC // ZR

    def z_part(ref, zz):
        return ref.at[lax.div(zz, per_blk), :, pl.ds(pl.multiple_of(lax.rem(zz, per_blk) * ZR, ZR), ZR), :]

    h_z = [send(z_part(hz, zs_[d]), hzr.at[d - 1], z_peer[d]) for d in range(1, NZ)]

    def r2():
        landed(r_z)
        rx[x] = pack_rows(*merge_rows(rz, 0, NZ))
        return [send(rx.at[x], rx.at[x], x_peer[d]) for d in range(1, NX)]

    def r3(r_x):
        landed(r_x)
        ry[y] = pack_rows(*merge_rows(rx, 0, NX))
        return [send(ry.at[y], ry.at[y], y_peer[d]) for d in range(1, NY)]

    def r4(r_y):
        landed(r_y)
        logp = []
        for s_ in range(2):
            m, s, pick = merge_rows(ry, s_ * NYL, (s_ + 1) * NYL)
            logp.append(pick - m - jnp.log(s))
        live = rowinfo[0:1, pl.ds(pl.multiple_of(tok * 256, 256), 256)].astype(F32)
        rc[tok] = jnp.broadcast_to(BETA * live * (logp[0] - logp[1]), (8, 256))
        return [send(rc.at[tok], rc.at[tok], core_peer)]

    def first_token(c):
        return pl.multiple_of(lax.div(z, per_blk) * HALF + RC * c + lax.rem(z, per_blk) * ZR, ZR)

    def r5(r_c):
        landed(r_c)
        row = jnp.concatenate([rc[0], rc[1]], axis=1)
        rew[...] = row
        spot = lax.broadcasted_iota(jnp.int32, (ZR, 512), 1)
        block = spot // 256
        inside = spot - 256 * block
        token = block * HALF + inside
        for c in range(NCH):
            t0 = first_token(c)
            mine = t0 + lax.broadcasted_iota(jnp.int32, (ZR, 512), 0)
            info = colinfo[pl.ds(t0, ZR), :]
            same = (info[:, 2:3] == rowinfo[1:2, :]) & (token >= mine) & (inside < HALF)
            ret = jnp.sum(jnp.where(same, row[:ZR], 0.0), axis=1, keepdims=True)
            wv[c] = jnp.broadcast_to(ret * info[:, 1:2].astype(F32), (ZR, LANES))

    def h3():
        landed(h_z)
        total = z_part(hz, z)[...]
        for d in range(1, NZ):
            total = total + hzr[d - 1]
        hfin[...] = total

    live_copies = {}

    def stage_a(c):
        landed([side_p[c]])
        rows = pl.ds(pl.multiple_of(own + RC * c, RC), RC)
        q = qr[pl.ds(RC * c, RC), :].astype(jnp.int32).astype(F32)
        scale = jnp.exp(q[:, vp - 1:vp] * STEP) * (1.0 / FULL)
        logit = jnp.where(lane < v, pp[rows, :] + q * scale, LOW)
        m = jnp.max(logit, axis=1, keepdims=True)
        e = jnp.exp(logit - m)
        is_target = (lane + first == colinfo[rows, 0:1]) & (lane < v)
        e_rest = jnp.where(is_target, 0.0, e)
        s_rest = jnp.sum(e_rest, axis=1, keepdims=True)
        s_target = jnp.sum(jnp.where(is_target, e, 0.0), axis=1, keepdims=True)
        eb[rows, :] = e_rest.astype(eb.dtype)
        st[rows, :] = jnp.where(st_lane == 0, m, jnp.where(st_lane == 1, s_rest, s_target))
        live_copies["e", c] = [
            send(eb.at[rows, :], eb.at[rows, :], core_peer),
            send(st.at[rows, :], st.at[rows, :], core_peer),
        ]

    def stage_b(c):
        landed(live_copies["e", c])
        r0, r1 = RC * c, HALF + RC * c
        e = jnp.concatenate([eb[r0:r0 + RC, :v], eb[r1:r1 + RC, :v]], axis=0)
        s = jnp.concatenate([st[r0:r0 + RC, :], st[r1:r1 + RC, :]], axis=0)
        g = nt_dot(e, pw[...])
        for i in range(NX):
            gs[c, i, 0] = g[:, LANES * i:LANES * (i + 1)]
            gs[c, i, 1] = s
        live_copies["x", c] = [send(gs.at[c, xs[d]], xr.at[c, d - 1], x_peer[d]) for d in range(1, NX)]

    def merge(gl, sl):
        m = sl[0][:, 0:1]
        for s in sl[1:]:
            m = jnp.maximum(m, s[:, 0:1])
        g_all = s_all = None
        for g, s in zip(gl, sl):
            a = jnp.exp(s[:, 0:1] - m)
            g_all = a * g if g_all is None else g_all + a * g
            s_all = a * s if s_all is None else s_all + a * s
        ln = lax.broadcasted_iota(jnp.int32, s_all.shape, 1)
        return g_all, jnp.where(ln == 0, m, s_all)

    def stage_c(c):
        landed(live_copies["x", c])
        gl = [gs[c, x, 0]] + [xr[c, d, 0] for d in range(NX - 1)]
        sl = [gs[c, x, 1]] + [xr[c, d, 1] for d in range(NX - 1)]
        g, s = merge(gl, sl)
        zs[c, 0] = g
        zs[c, 1] = s
        live_copies["z", c] = [
            send(zs.at[c, :, pl.ds(pl.multiple_of(zs_[d] * ZR, ZR), ZR), :], zr.at[c, d - 1], z_peer[d])
            for d in range(1, NZ)
        ]

    def stage_d(c):
        landed(live_copies["z", c])
        mine = pl.ds(pl.multiple_of(z * ZR, ZR), ZR)
        gl = [zs[c, 0, mine, :]] + [zr[c, d, 0] for d in range(NZ - 1)]
        sl = [zs[c, 1, mine, :]] + [zr[c, d, 1] for d in range(NZ - 1)]
        g, s = merge(gl, sl)
        yr[c, ylo, 0] = g
        yr[c, ylo, 1] = s
        yr[c, ylo, 2] = hfin[c]
        live_copies["y", c] = [send(yr.at[c, ylo], yr.at[c, ylo], yl_peer[d]) for d in range(1, NYL)]

    def stage_e(c):
        landed(live_copies["y", c])
        g, s = merge([yr[c, i, 0] for i in range(NYL)], [yr[c, i, 1] for i in range(NYL)])
        h = yr[c, 0, 2]
        for i in range(1, NYL):
            h = h + yr[c, i, 2]
        rest, target = s[:, 1:2], s[:, 2:3]
        scale = wv[c] / (rest + target)
        mine = pl.ds(pl.multiple_of(z * ZR, ZR), ZR)
        zag[c, mine, :] = scale * (g - rest * h)
        live_copies["zag", c] = [send(zag.at[c, mine, :], zag.at[c, mine, :], z_peer[d]) for d in range(1, NZ)]

    def stage_f(c):
        landed(live_copies["zag", c])
        hx[c, x] = zag[c].astype(hx.dtype)
        live_copies["xag", c] = [send(hx.at[c, x], hx.at[c, x], x_peer[d]) for d in range(1, NX)]

    def stage_g(c):
        landed(live_copies["xag", c])
        for i in range(NX):
            for b in range(2):
                hg[HALF * b + RC * c:HALF * b + RC * (c + 1), LANES * i:LANES * (i + 1)] = hx[c, i, RC * b:RC * (b + 1), :]

    r_x = r2()
    r_y = r_c = None
    stages = [stage_c, stage_d, stage_e, stage_f, stage_g]
    for k in range(NCH + 5):
        if k < NCH:
            stage_a(k)
        if k == 1:
            r_y = r3(r_x)
        if k == 2:
            r_c = r4(r_y)
            h3()
        if k == 3:
            r5(r_c)
        for j in range(2):
            if 0 <= k - 1 - j < NCH:
                stages[j](k - 1 - j)
            if j == 0 and k < NCH:
                stage_b(k)
        for j in range(2, 5):
            if 0 <= k - 1 - j < NCH:
                stages[j](k - 1 - j)
    for c in copies:
        c.wait_send()


def per_device(rh, rw, ph, pw, targets, mask, ids):
    v = rw.shape[2]
    feats, depth = ph.shape[1], rh.shape[2]
    vp = -(-v // LANES) * LANES
    if vp == v:
        vp += LANES
    info = jnp.stack([targets, mask, ids], axis=1)
    colinfo = jnp.pad(info, ((0, 0), (0, LANES - 3)))
    rowinfo = jnp.pad(jnp.stack([mask, ids]).reshape(2, 2, HALF), ((0, 6), (0, 0), (0, 256 - HALF)))
    rowinfo = rowinfo.reshape(8, 512)
    bf, i16 = jnp.bfloat16, jnp.int16
    vm = pltpu.VMEM
    scratch = [
        vm((W, depth), bf), vm((depth, v), bf), vm((W, feats), bf), vm((feats, v), bf),
        vm((W, vp), F32), vm((HALF, vp), F32), vm((HALF, vp), i16), vm((HALF, vp), i16),
        vm((W, vp), bf), vm((W, LANES), F32),
        vm((W, vp), F32), vm((HALF, vp), F32),
        vm((NCH, NX, 2, CR, LANES), F32), vm((NCH, NX - 1, 2, CR, LANES), F32),
        vm((NCH, 2, CR, LANES), F32), vm((NCH, NZ - 1, 2, ZR, LANES), F32),
        vm((NCH, NYL, 3, ZR, LANES), F32), vm((NCH, CR, LANES), F32), vm((NCH, NX, CR, LANES), bf),
        vm((NX, W, LANES), bf), vm((NX - 1, W, LANES), bf), vm((2, NCH, RC, LANES), F32),
        vm((NZ - 1, NCH, ZR, LANES), F32), vm((NCH, ZR, LANES), F32),
        vm((NZ, 8, 256), F32), vm((NX, 8, 256), F32), vm((NY, 8, 256), F32), vm((2, 8, 256), F32),
        vm((NCH, ZR, LANES), F32),
        pltpu.SemaphoreType.DMA((4,)), pltpu.SemaphoreType.DMA((NSEM,)), pltpu.SemaphoreType.DMA((NSEM,)),
    ]
    anyspec = pl.BlockSpec(memory_space=pl.ANY)
    vspec = pl.BlockSpec(memory_space=pltpu.VMEM)
    rew, hg = pl.pallas_call(
        functools.partial(kernel, v),
        out_shape=(jax.ShapeDtypeStruct((8, 512), F32), jax.ShapeDtypeStruct((W, feats), bf)),
        in_specs=[anyspec] * 4 + [vspec] * 2,
        out_specs=(vspec, vspec),
        scratch_shapes=scratch,
        compiler_params=pltpu.CompilerParams(
            collective_id=0, has_side_effects=True, vmem_limit_bytes=56 << 20
        ),
    )(rh, rw, ph, pw, colinfo, rowinfo)
    rewards = jnp.concatenate([rew[0, :HALF], rew[0, 256:256 + HALF]])
    return rewards, hg


def solution(mesh):
    placed = (
        P("side", None, "tok"),
        P("side", "tok", "vocab"),
        P(None, ("side", "tok")),
        P(("side", "tok"), "vocab"),
        P(),
        P(),
        P(),
    )
    return jax.shard_map(
        per_device,
        mesh=mesh,
        in_specs=placed,
        out_specs=(P(), P(None, ("side", "tok"))),
        check_vma=False,
    )
```

time: 1580 us -> 94.4 us (0.06)
  the two profiles are of different devices: /device:TPU:32 before, /device:TPU:24 now
where the time goes in v1:
time: 94.4 us; the launch traced here: 94 us
  Pallas kernels  80 us (85%)
  local copies, waits for them, and re-layouts  12.7 us (13%)
    pallas_call x1, Pallas kernels, per_device(): pl.pallas_call(functools.partial(kernel, v), out_shape=(jax.ShapeDtypeStr...  80 us
    unnamed x5, local copies, waits for them, and re-layouts  6.79 us
    another operation x4, local copies, waits for them, and re-layouts, per_device(): info = jnp.stack([targets, mask, ids], axis=1)  2.33 us

profile of v1, /device:TPU:24, one launch (start us, length us, event | category | flops | bytes accessed | tf_op | source)
XLA Modules:
  0.0 94.0 jit_solution(12803948476137598050)
XLA Ops:
  0.6 0.0 copy-start
  0.6 0.8 stack.21
  1.5 0.7 stack.22
  2.2 0.7 stack.23
  2.9 0.8 stack.25
  3.6 0.8 stack.26
  4.4 0.6 pad.9
  5.0 0.1 copy.16
  5.1 0.7 pad.8.colinfo
  5.8 2.4 %copy.18.pw_hbm = bf16[512,1187]{1,0:T(8,128)(2,1)} copy(bf16[512,1187]{0,1:T(8,128)(2,1)} %param.10) | data formatting | bytes 2430976 | tf_op args[3]
  8.2 0.0 copy-done
  8.2 2.7 %copy.17.rw_hbm = bf16[1,1024,1187]{2,1,0:T(8,128)(2,1)} copy(bf16[1,1024,1187]{1,2,0:T(8,128)(2,1)S(1)} %copy-done) | data formatting | bytes 4861952 | tf_op args[1]
  10.9 80.0 %shard_map.86 = (f32[8,512]{1,0:T(8,128)}, bf16[320,512]{1,0:T(8,128)(2,1)}) custom-call(bf16[1,320,1024]{2,1,0:T(8,128)(2,1)} %rh_hbm.1, bf16[1,1024,1187]{2,1,0:T(8,128)(2,1)} %copy.17.rw_hbm, bf16[320,512]{1,0:T(8,128)(2,1)} %ph_hbm.1, bf16[512,1187]{1,0:T(8,128)(2,1)} %copy.18.pw_hbm, s32[320,128]{1,0:T(8,128)} %pad.8.colinfo, s32[8,512]{1,0:T(8,128)} %bitcast.3), custom_call_target="tpu_custom_call" | custom-call | tf_op jit(solution)/shard_map/pallas_call | solution.py:374
  90.9 0.7 fusion
  91.7 0.7 pad_maximum_fusion
  92.3 1.7 %copy.20 = bf16[320,512]{1,0:T(8,128)(2,1)} copy(bf16[320,512]{1,0:T(8,128)(2,1)} %get-tuple-element.11) | data formatting | bytes 655360
  (2 shorter events, 0.0 us)
Async XLA Ops:
  0.6 7.6 %copy-start = (bf16[1,1024,1187]{1,2,0:T(8,128)(2,1)S(1)}, bf16[1,1024,1187]{1,2,0:T(8,128)(2,1)}, u32[]{:S(2)}) copy-start(bf16[1,1024,1187]{1,2,0:T(8,128)(2,1)} %param.8) | copy-start | bytes 7292932

commit v2 on v1

v2 whole, which is shorter than its diff:
```python
import functools
import math

import jax
import jax.numpy as jnp
from jax import lax
from jax.experimental import pallas as pl
from jax.experimental.pallas import tpu as pltpu
from jax.sharding import PartitionSpec as P

BETA = 0.05
MESH = pl.DeviceIdType.MESH
F32 = jnp.float32
NX, NYL, NZ = 4, 4, 8
NY = 2 * NYL
W = 320
HALF = 160
RC = 32
NCH = HALF // RC
SR = 16
WINDOW = 4
CR = 2 * RC
ZR = CR // NZ
LANES = 128
STEP = math.log(2.0) / 16.0
FULL = 32700.0
LOW = -1e30
NSEM = 256


def nt_dot(a, b):
    return lax.dot_general(a, b, (((1,), (1,)), ((), ())), preferred_element_type=F32)


def kernel(
    v,
    rh_hbm, rw_hbm, ph_hbm, pw_hbm, t_hbm, m_hbm, i_hbm,
    rew, hg,
    rh, rw, ph, pw, pp, pr, qs, qr, eb, st,
    rp, rr, gs, xr, zs, zr, yr, zag, hx,
    hs, hxr, hz, hzr, hfin, rz, rx, ry, rc, wv, colinfo, rowinfo, targets, mask, ids,
    load_sem, send_sem, recv_sem,
):
    vp = pp.shape[1]
    feats = ph.shape[1]
    side = lax.axis_index("side")
    vocab = lax.axis_index("vocab")
    tok = lax.axis_index("tok")
    ylo = lax.div(vocab, NX * NZ)
    x = lax.rem(lax.div(vocab, NZ), NX)
    z = lax.rem(vocab, NZ)
    y = side * NYL + ylo
    first = vocab * v

    def at(yy, xx, zz, tt):
        return (lax.div(yy, NYL), lax.rem(yy, NYL) * (NX * NZ) + xx * NZ + zz, tt)

    core_peer = at(y, x, z, 1 - tok)
    side_peer = at(lax.rem(y + NYL, NY), x, z, tok)
    xs = [lax.rem(x + d, NX) for d in range(NX)]
    zs_ = [lax.rem(z + d, NZ) for d in range(NZ)]
    x_peer = [at(y, xs[d], z, tok) for d in range(NX)]
    z_peer = [at(y, x, zs_[d], tok) for d in range(NZ)]
    y_peer = [at(lax.rem(y + d, NY), x, z, tok) for d in range(NY)]
    yls = [lax.rem(ylo + d, NYL) for d in range(NYL)]
    yl_peer = [at(side * NYL + yls[d], x, z, tok) for d in range(NYL)]

    loads = []

    def load(src, dst, pieces=1):
        step = -(-src.shape[0] // (16 * pieces)) * 16
        group = []
        for r in range(0, src.shape[0], step):
            part = pl.ds(r, min(step, src.shape[0] - r))
            group.append(pltpu.make_async_copy(src.at[part], dst.at[part], load_sem.at[len(loads)]))
            loads.append(group[-1])
            group[-1].start()
        return group

    def loaded(group):
        for c in group:
            c.wait()

    policy = load(pw_hbm, pw, 4) + load(ph_hbm, ph)
    lists_in = [load(t_hbm, targets), load(m_hbm, mask), load(i_hbm, ids)]

    barrier = pltpu.get_barrier_semaphore()
    peers = [core_peer] + x_peer[1:] + z_peer[1:] + y_peer[1:]
    for p in peers:
        pl.semaphore_signal(barrier, inc=1, device_id=p, device_id_type=MESH)

    copies = []

    def send(src, dst, peer):
        i = len(copies)
        c = pltpu.make_async_remote_copy(
            src_ref=src, dst_ref=dst, send_sem=send_sem.at[i], recv_sem=recv_sem.at[i],
            device_id=peer, device_id_type=MESH,
        )
        c.start()
        copies.append(c)
        return c

    def landed(group):
        for c in group:
            c.wait_recv()

    for c in lists_in:
        loaded(c)
    lists = [r[...].reshape(1, W) for r in (targets, mask, ids)]
    rows3 = jnp.concatenate(lists + [jnp.zeros((5, W), jnp.int32)], axis=0).astype(F32)
    rows3 = jnp.concatenate([rows3, jnp.zeros((LANES - 8, W), F32)], axis=0)
    rows3 = jnp.concatenate([rows3, jnp.zeros((LANES, 384 - W), F32)], axis=1)
    colinfo[...] = jnp.transpose(rows3)[:W].astype(jnp.int32)
    for b in range(2):
        half = jnp.concatenate([r[:, HALF * b:HALF * (b + 1)] for r in lists[1:]], axis=0)
        rowinfo[0:2, 256 * b:256 * b + HALF] = half
        rowinfo[0:2, 256 * b + HALF:256 * (b + 1)] = jnp.zeros((2, 256 - HALF), jnp.int32)

    tail = vp - LANES
    for buf in (pp, rp):
        buf[:, tail:] = jnp.zeros((W, LANES), F32)
    eb[:, tail:] = jnp.zeros((W, LANES), eb.dtype)

    own = pl.multiple_of(tok * HALF, HALF)
    other = pl.multiple_of((1 - tok) * HALF, HALF)

    loaded(policy)
    reward = load(rh_hbm.at[0], rh) + load(rw_hbm.at[0], rw, 4)
    pp[pl.ds(other, HALF), :v] = nt_dot(ph[pl.ds(other, HALF), :], pw[...])
    pl.semaphore_wait(barrier, len(peers))
    core_p = []
    for c in range(NCH):
        core_p.append(send(pp.at[pl.ds(other + RC * c, RC), :], pr.at[pl.ds(RC * c, RC), :], core_peer))
    pp[pl.ds(own, HALF), :v] = nt_dot(ph[pl.ds(own, HALF), :], pw[...])

    lane = lax.broadcasted_iota(jnp.int32, (RC, vp), 1)
    st_lane = lax.broadcasted_iota(jnp.int32, (RC, LANES), 1)

    side_p = []

    def side_send():
        rows = pl.ds(SR * len(side_p), SR)
        side_p.append(send(qs.at[rows, :], qr.at[rows, :], side_peer))

    def side_step(i):
        landed([side_p[i]])
        if len(side_p) < HALF // SR:
            side_p[i].wait_send()
            waited.append(side_p[i])
            side_send()

    waited = []
    for c in range(NCH):
        landed([core_p[c]])
        rows = pl.ds(pl.multiple_of(own + RC * c, RC), RC)
        part = pp[rows, :] + pr[pl.ds(RC * c, RC), :]
        pp[rows, :] = part
        top = jnp.maximum(jnp.max(jnp.abs(part), axis=1, keepdims=True), 1e-6)
        expo = jnp.ceil(jnp.log(top) / STEP)
        inv = FULL * jnp.exp(expo * -STEP)
        quant = jnp.clip(jnp.round(part * inv), -32767.0, 32767.0)
        quant = jnp.where(lane == vp - 1, expo, quant)
        qs[pl.ds(RC * c, RC), :] = quant.astype(jnp.int32).astype(jnp.int16)
        for _ in range(2):
            if len(side_p) < WINDOW:
                side_send()

    wide = lax.broadcasted_iota(jnp.int32, (W, v), 1) + first
    hot = (wide == colinfo[:, 0:1]).astype(jnp.bfloat16)
    picked = jnp.dot(hot, pw[...], preferred_element_type=F32).astype(jnp.bfloat16)
    for i in range(NX):
        hs[i] = picked[:, LANES * i:LANES * (i + 1)]
    h_x = [send(hs.at[xs[d]], hxr.at[d - 1], x_peer[d]) for d in range(1, NX)]

    loaded(reward)
    rp[pl.ds(other, HALF), :v] = nt_dot(rh[pl.ds(other, HALF), :], rw[...])
    core_r = send(rp.at[pl.ds(other, HALF), :], rr, core_peer)
    rp[pl.ds(own, HALF), :v] = nt_dot(rh[pl.ds(own, HALF), :], rw[...])
    def r1():
        landed([core_r])
        stats = []
        for c in range(NCH):
            rows = pl.ds(pl.multiple_of(own + RC * c, RC), RC)
            logit = rp[rows, :] + rr[pl.ds(RC * c, RC), :]
            logit = jnp.where(lane < v, logit, LOW)
            m = jnp.max(logit, axis=1, keepdims=True)
            s = jnp.sum(jnp.exp(logit - m), axis=1, keepdims=True)
            is_target = (lane + first == colinfo[rows, 0:1]) & (lane < v)
            pick = jnp.sum(jnp.where(is_target, logit, 0.0), axis=1, keepdims=True)
            stats.append(jnp.where(st_lane == 0, m, jnp.where(st_lane == 1, s, jnp.where(st_lane == 2, pick, 0.0))))
        stats.append(jnp.zeros((256 - HALF, LANES), F32))
        rz[z] = jnp.transpose(jnp.concatenate(stats, axis=0))[:8, :]
        return [send(rz.at[z], rz.at[z], z_peer[d]) for d in range(1, NZ)]

    def merge_rows(buf, lo, hi):
        tiles = [buf[i] for i in range(lo, hi)]
        m = tiles[0][0:1]
        for t in tiles[1:]:
            m = jnp.maximum(m, t[0:1])
        s = jnp.zeros_like(m)
        pick = jnp.zeros_like(m)
        for t in tiles:
            s = s + jnp.exp(t[0:1] - m) * t[1:2]
            pick = pick + t[2:3]
        return m, s, pick

    def pack_rows(m, s, pick):
        row = lax.broadcasted_iota(jnp.int32, (8, 256), 0)
        return jnp.where(row == 0, m, jnp.where(row == 1, s, jnp.where(row == 2, pick, 0.0)))

    def h2():
        landed(h_x)
        h_own = hs[x].astype(F32)
        for d in range(1, NX):
            h_own = h_own + hxr[d - 1].astype(F32)
        hz[...] = h_own.reshape(2, NCH, RC, LANES)
        return [send(z_part(hz, zs_[d]), hzr.at[d - 1], z_peer[d]) for d in range(1, NZ)]

    per_blk = RC // ZR

    def z_part(ref, zz):
        return ref.at[lax.div(zz, per_blk), :, pl.ds(pl.multiple_of(lax.rem(zz, per_blk) * ZR, ZR), ZR), :]

    def r2(r_z):
        landed(r_z)
        rx[x] = pack_rows(*merge_rows(rz, 0, NZ))
        return [send(rx.at[x], rx.at[x], x_peer[d]) for d in range(1, NX)]

    def r3(r_x):
        landed(r_x)
        ry[y] = pack_rows(*merge_rows(rx, 0, NX))
        return [send(ry.at[y], ry.at[y], y_peer[d]) for d in range(1, NY)]

    def r4(r_y):
        landed(r_y)
        logp = []
        for s_ in range(2):
            m, s, pick = merge_rows(ry, s_ * NYL, (s_ + 1) * NYL)
            logp.append(pick - m - jnp.log(s))
        live = rowinfo[0:1, pl.ds(pl.multiple_of(tok * 256, 256), 256)].astype(F32)
        rc[tok] = jnp.broadcast_to(BETA * live * (logp[0] - logp[1]), (8, 256))
        return [send(rc.at[tok], rc.at[tok], core_peer)]

    def r5(r_c):
        landed(r_c)
        row = jnp.concatenate([rc[0], rc[1]], axis=1)
        rew[...] = jnp.concatenate([rc[0, 0:1, :HALF], rc[1, 0:1, :HALF]], axis=1).reshape(W)
        spot = lax.broadcasted_iota(jnp.int32, (RC, 512), 1)
        block = spot // 256
        inside = spot - 256 * block
        token = block * HALF + inside
        for t0 in range(0, W, RC):
            mine = t0 + lax.broadcasted_iota(jnp.int32, (RC, 512), 0)
            info = colinfo[t0:t0 + RC, :]
            same = (info[:, 2:3] == rowinfo[1:2, :]) & (token >= mine) & (inside < HALF)
            ret = jnp.sum(jnp.where(same, row[0:1], 0.0), axis=1, keepdims=True)
            wv[t0:t0 + RC, :] = jnp.broadcast_to(ret * info[:, 1:2].astype(F32), (RC, LANES))

    def h3(h_z):
        landed(h_z)
        total = z_part(hz, z)[...]
        for d in range(1, NZ):
            total = total + hzr[d - 1]
        hfin[...] = total

    live_copies = {}

    def stage_a(c):
        rows = pl.ds(pl.multiple_of(own + RC * c, RC), RC)
        q = qr[pl.ds(RC * c, RC), :].astype(jnp.int32).astype(F32)
        scale = jnp.exp(q[:, vp - 1:vp] * STEP) * (1.0 / FULL)
        logit = jnp.where(lane < v, pp[rows, :] + q * scale, LOW)
        m = jnp.max(logit, axis=1, keepdims=True)
        e = jnp.exp(logit - m)
        is_target = (lane + first == colinfo[rows, 0:1]) & (lane < v)
        e_rest = jnp.where(is_target, 0.0, e)
        s_rest = jnp.sum(e_rest, axis=1, keepdims=True)
        s_target = jnp.sum(jnp.where(is_target, e, 0.0), axis=1, keepdims=True)
        eb[rows, :] = e_rest.astype(eb.dtype)
        st[rows, :] = jnp.where(st_lane == 0, m, jnp.where(st_lane == 1, s_rest, s_target))
        live_copies["e", c] = [
            send(eb.at[rows, :], eb.at[rows, :], core_peer),
            send(st.at[rows, :], st.at[rows, :], core_peer),
        ]

    def split3(s, ref):
        ln = lax.broadcasted_iota(jnp.int32, s.shape, 1)
        left = jnp.where(ln < 3, s[:, 0:1], jnp.where(ln < 6, s[:, 1:2], s[:, 2:3]))
        part = lax.rem(ln, 3)
        for i in range(2):
            ref[...] = left.astype(ref.dtype)
            left = jnp.where(part > i, left - ref[...].astype(F32), left)
        ref[...] = left.astype(ref.dtype)

    def stage_b(c):
        landed(live_copies["e", c])
        r0, r1 = RC * c, HALF + RC * c
        e = jnp.concatenate([eb[r0:r0 + RC, :v], eb[r1:r1 + RC, :v]], axis=0)
        split3(jnp.concatenate([st[r0:r0 + RC, :], st[r1:r1 + RC, :]], axis=0), gs.at[c, 0, 1])
        s = gs[c, 0, 1]
        g = jnp.dot(e, pw[...], preferred_element_type=F32)
        for i in range(NX):
            gs[c, i, 0] = g[:, LANES * i:LANES * (i + 1)].astype(gs.dtype)
            if i:
                gs[c, i, 1] = s
        live_copies["x", c] = [send(gs.at[c, xs[d]], xr.at[c, d - 1], x_peer[d]) for d in range(1, NX)]

    def merge(gl, sl):
        m = sl[0][:, 0:1]
        for s in sl[1:]:
            m = jnp.maximum(m, s[:, 0:1])
        g_all = s_all = None
        for g, s in zip(gl, sl):
            a = jnp.exp(s[:, 0:1] - m)
            g_all = a * g if g_all is None else g_all + a * g
            s_all = a * s if s_all is None else s_all + a * s
        ln = lax.broadcasted_iota(jnp.int32, s_all.shape, 1)
        return g_all, jnp.where(ln == 0, m, s_all)

    def merge_parts(gl, tl):
        tl = [t.astype(F32) for t in tl]
        ml = [t[:, 0:1] + t[:, 1:2] + t[:, 2:3] for t in tl]
        m = ml[0]
        for other_m in ml[1:]:
            m = jnp.maximum(m, other_m)
        g_all = t_all = None
        for g, t, mi in zip(gl, tl, ml):
            a = jnp.exp(mi - m)
            g = a * g.astype(F32)
            t = a * t
            g_all = g if g_all is None else g_all + g
            t_all = t if t_all is None else t_all + t
        ln = lax.broadcasted_iota(jnp.int32, t_all.shape, 1)
        r, s = (t_all[:, i:i + 1] + t_all[:, i + 1:i + 2] + t_all[:, i + 2:i + 3] for i in (3, 6))
        return g_all, jnp.where(ln == 0, m, jnp.where(ln == 1, r, s))

    def stage_c(c):
        landed(live_copies["x", c])
        gl = [gs[c, x, 0]] + [xr[c, d, 0] for d in range(NX - 1)]
        tl = [gs[c, x, 1]] + [xr[c, d, 1] for d in range(NX - 1)]
        g, s = merge_parts(gl, tl)
        zs[c, 0] = g
        zs[c, 1] = s
        live_copies["z", c] = [
            send(zs.at[c, :, pl.ds(pl.multiple_of(zs_[d] * ZR, ZR), ZR), :], zr.at[c, d - 1], z_peer[d])
            for d in range(1, NZ)
        ]

    def stage_d(c):
        landed(live_copies["z", c])
        mine = pl.ds(pl.multiple_of(z * ZR, ZR), ZR)
        gl = [zs[c, 0, mine, :]] + [zr[c, d, 0] for d in range(NZ - 1)]
        sl = [zs[c, 1, mine, :]] + [zr[c, d, 1] for d in range(NZ - 1)]
        g, s = merge(gl, sl)
        yr[c, ylo, 0] = g
        yr[c, ylo, 1] = s
        yr[c, ylo, 2] = hfin[c]
        live_copies["y", c] = [send(yr.at[c, ylo], yr.at[c, ylo], yl_peer[d]) for d in range(1, NYL)]

    def stage_e(c):
        landed(live_copies["y", c])
        g, s = merge([yr[c, i, 0] for i in range(NYL)], [yr[c, i, 1] for i in range(NYL)])
        h = yr[c, 0, 2]
        for i in range(1, NYL):
            h = h + yr[c, i, 2]
        rest, target = s[:, 1:2], s[:, 2:3]
        scale = 1.0 / (rest + target)
        mine = pl.ds(pl.multiple_of(z * ZR, ZR), ZR)
        zag[c, mine, :] = scale * (g - rest * h)
        live_copies["zag", c] = [send(zag.at[c, mine, :], zag.at[c, mine, :], z_peer[d]) for d in range(1, NZ)]

    def stage_f(c):
        landed(live_copies["zag", c])
        weight = jnp.concatenate([wv[RC * c:RC * (c + 1), :], wv[HALF + RC * c:HALF + RC * (c + 1), :]], axis=0)
        hx[c, x] = (weight * zag[c]).astype(hx.dtype)
        live_copies["xag", c] = [send(hx.at[c, x], hx.at[c, x], x_peer[d]) for d in range(1, NX)]

    def stage_g(c):
        landed(live_copies["xag", c])
        for i in range(NX):
            for b in range(2):
                hg[HALF * b + RC * c:HALF * b + RC * (c + 1), LANES * i:LANES * (i + 1)] = hx[c, i, RC * b:RC * (b + 1), :]

    chain = {
        "S": side_step, "A": stage_a, "B": stage_b, "C": stage_c, "D": stage_d, "E": stage_e, "F": stage_f, "G": stage_g,
    }
    order = (
        "S0", "r1", "S1", "A0", "B0", "S2", "h2", "S3", "A1", "B1", "C0", "r2", "S4", "S5", "A2",
        "B2", "C1", "h3", "D0", "r3", "S6", "S7", "A3", "B3", "C2", "D1", "E0", "S8", "S9", "A4",
        "B4", "C3", "D2", "E1", "r4", "C4", "D3", "E2", "r5", "F0", "D4", "E3", "F1", "G0", "E4",
        "F2", "G1", "F3", "G2", "F4", "G3", "G4",
    )
    for word in order:
        if word == "h2":
            h_z = h2()
        elif word == "h3":
            h3(h_z)
        elif word == "r1":
            r_z = r1()
        elif word == "r2":
            r_x = r2(r_z)
        elif word == "r3":
            r_y = r3(r_x)
        elif word == "r4":
            r_c = r4(r_y)
        elif word == "r5":
            r5(r_c)
        else:
            chain[word[0]](int(word[1:]))
    for c in copies:
        if all(c is not w for w in waited):
            c.wait_send()


def hand_over(rew, hg, rew_out, hg_out):
    rew_out[...] = rew[...]
    hg_out[...] = hg[...]


def per_device(rh, rw, ph, pw, targets, mask, ids):
    v = rw.shape[2]
    rw, pw = jnp.swapaxes(rw, 1, 2), jnp.swapaxes(pw, 0, 1)
    feats, depth = ph.shape[1], rh.shape[2]
    vp = -(-v // LANES) * LANES
    if vp == v:
        vp += LANES
    bf, i16 = jnp.bfloat16, jnp.int16
    vm = pltpu.VMEM
    scratch = [
        vm((W, depth), bf), vm((v, depth), bf), vm((W, feats), bf), vm((v, feats), bf),
        vm((W, vp), F32), vm((HALF, vp), F32), vm((HALF, vp), i16), vm((HALF, vp), i16),
        vm((W, vp), bf), vm((W, LANES), F32),
        vm((W, vp), F32), vm((HALF, vp), F32),
        vm((NCH, NX, 2, CR, LANES), bf), vm((NCH, NX - 1, 2, CR, LANES), bf),
        vm((NCH, 2, CR, LANES), F32), vm((NCH, NZ - 1, 2, ZR, LANES), F32),
        vm((NCH, NYL, 3, ZR, LANES), F32), vm((NCH, CR, LANES), F32), vm((NCH, NX, CR, LANES), bf),
        vm((NX, W, LANES), bf), vm((NX - 1, W, LANES), bf), vm((2, NCH, RC, LANES), F32),
        vm((NZ - 1, NCH, ZR, LANES), F32), vm((NCH, ZR, LANES), F32),
        vm((NZ, 8, 256), F32), vm((NX, 8, 256), F32), vm((NY, 8, 256), F32), vm((2, 8, 256), F32),
        vm((W, LANES), F32), vm((W, LANES), jnp.int32), vm((8, 512), jnp.int32),
        vm((W,), jnp.int32), vm((W,), jnp.int32), vm((W,), jnp.int32),
        pltpu.SemaphoreType.DMA((16,)), pltpu.SemaphoreType.DMA((NSEM,)), pltpu.SemaphoreType.DMA((NSEM,)),
    ]
    vspec = pl.BlockSpec(memory_space=pltpu.VMEM)
    hspec = pl.BlockSpec(memory_space=pltpu.HBM)
    rew, hg = pl.pallas_call(
        functools.partial(kernel, v),
        out_shape=(jax.ShapeDtypeStruct((W,), F32), jax.ShapeDtypeStruct((W, feats), bf)),
        in_specs=[hspec] * 7,
        out_specs=(vspec, vspec),
        scratch_shapes=scratch,
        compiler_params=pltpu.CompilerParams(
            collective_id=0, has_side_effects=True, vmem_limit_bytes=60 << 20
        ),
    )(rh, rw, ph, pw, targets, mask, ids)
    return pl.pallas_call(
        hand_over,
        out_shape=(jax.ShapeDtypeStruct((W,), F32), jax.ShapeDtypeStruct((W, feats), bf)),
        in_specs=[vspec, vspec],
        out_specs=(vspec, vspec),
    )(rew, hg)


def solution(mesh):
    placed = (
        P("side", None, "tok"),
        P("side", "tok", "vocab"),
        P(None, ("side", "tok")),
        P(("side", "tok"), "vocab"),
        P(),
        P(),
        P(),
    )
    return jax.shard_map(
        per_device,
        mesh=mesh,
        in_specs=placed,
        out_specs=(P(), P(None, ("side", "tok"))),
        check_vma=False,
    )
```

time: 94.4 us -> 70.9 us (0.75)
  the two profiles are of different devices: /device:TPU:24 before, /device:TPU:2 now
where the time goes in v2:
time: 70.9 us; the launch traced here: 70.8 us
  Pallas kernels  70.1 us (99%)
    pallas_call x1, Pallas kernels, per_device(): pl.pallas_call(functools.partial(kernel, v), out_shape=(jax.ShapeDtypeStr...  68.4 us
    pallas_call x1, Pallas kernels, per_device(): pl.pallas_call(hand_over, out_shape=(jax.ShapeDtypeStruct((W,), F32), jax...  1.73 us

profile of v2, /device:TPU:2, one launch (start us, length us, event | category | flops | bytes accessed | tf_op | source)
XLA Modules:
  0.0 70.8 jit_solution(6569639862445749676)
XLA Ops:
  0.6 68.4 %shard_map.86 = (f32[320]{0:T(512)}, bf16[320,512]{1,0:T(8,128)(2,1)}) custom-call(bf16[1,320,1024]{2,1,0:T(8,128)(2,1)} %rh_hbm.1, bf16[1,1187,1024]{2,1,0:T(8,128)(2,1)} %bitcast.2, bf16[320,512]{1,0:T(8,128)(2,1)} %ph_hbm.1, bf16[1187,512]{1,0:T(8,128)(2,1)} %bitcast.3, s32[320]{0:T(512)} %t_hbm.1, s32[320]{0:T(512)} %m_hbm.1, s32[320]{0:T(512)} %i_hbm.1), custom_call_target="tpu_custom_call" | custom-call | tf_op jit(solution)/shard_map/pallas_call | solution.py:447
  69.0 1.7 %shard_map.87 = (f32[320]{0:T(512)}, bf16[320,512]{1,0:T(8,128)(2,1)}) custom-call(f32[320]{0:T(512)} %get-tuple-element.4.rew, bf16[320,512]{1,0:T(8,128)(2,1)} %get-tuple-element.5.hg), custom_call_target="tpu_custom_call" | custom-call | tf_op jit(solution)/shard_map/pallas_call | solution.py:457

commit v3 on v2

--- a/solution.py
+++ b/solution.py
@@ -387,8 +387,8 @@
     }
     order = (
         "S0", "r1", "S1", "A0", "B0", "S2", "h2", "S3", "A1", "B1", "C0", "r2", "S4", "S5", "A2",
-        "B2", "C1", "h3", "D0", "r3", "S6", "S7", "A3", "B3", "C2", "D1", "E0", "S8", "S9", "A4",
-        "B4", "C3", "D2", "E1", "r4", "C4", "D3", "E2", "r5", "F0", "D4", "E3", "F1", "G0", "E4",
+        "B2", "C1", "h3", "D0", "r3", "S6", "S7", "A3", "B3", "C2", "D1", "S8", "S9", "A4", "B4",
+        "C3", "D2", "E0", "E1", "C4", "r4", "E2", "D3", "r5", "F0", "D4", "E3", "F1", "G0", "E4",
         "F2", "G1", "F3", "G2", "F4", "G3", "G4",
     )
     for word in order:

time: 70.9 us -> 70 us (0.987)
  the two profiles are of different devices: /device:TPU:2 before, /device:TPU:24 now
where the time goes in v3:
time: 70 us; the launch traced here: 69.8 us
  Pallas kernels  69.2 us (99%)
    pallas_call x1, Pallas kernels, per_device(): pl.pallas_call(functools.partial(kernel, v), out_shape=(jax.ShapeDtypeStr...  67.4 us
    pallas_call x1, Pallas kernels, per_device(): pl.pallas_call(hand_over, out_shape=(jax.ShapeDtypeStruct((W,), F32), jax...  1.73 us

profile of v3, /device:TPU:24, one launch (start us, length us, event | category | flops | bytes accessed | tf_op | source)
XLA Modules:
  0.0 69.8 jit_solution(4244338588158911644)
XLA Ops:
  0.6 67.4 %shard_map.86 = (f32[320]{0:T(512)}, bf16[320,512]{1,0:T(8,128)(2,1)}) custom-call(bf16[1,320,1024]{2,1,0:T(8,128)(2,1)} %rh_hbm.1, bf16[1,1187,1024]{2,1,0:T(8,128)(2,1)} %bitcast.2, bf16[320,512]{1,0:T(8,128)(2,1)} %ph_hbm.1, bf16[1187,512]{1,0:T(8,128)(2,1)} %bitcast.3, s32[320]{0:T(512)} %t_hbm.1, s32[320]{0:T(512)} %m_hbm.1, s32[320]{0:T(512)} %i_hbm.1), custom_call_target="tpu_custom_call" | custom-call | tf_op jit(solution)/shard_map/pallas_call | solution.py:447
  68.1 1.7 %shard_map.87 = (f32[320]{0:T(512)}, bf16[320,512]{1,0:T(8,128)(2,1)}) custom-call(f32[320]{0:T(512)} %get-tuple-element.4.rew, bf16[320,512]{1,0:T(8,128)(2,1)} %get-tuple-element.5.hg), custom_call_target="tpu_custom_call" | custom-call | tf_op jit(solution)/shard_map/pallas_call | solution.py:457

commit v4 on v3

--- a/solution.py
+++ b/solution.py
@@ -191,7 +191,7 @@
             stats.append(jnp.where(st_lane == 0, m, jnp.where(st_lane == 1, s, jnp.where(st_lane == 2, pick, 0.0))))
         stats.append(jnp.zeros((256 - HALF, LANES), F32))
         rz[z] = jnp.transpose(jnp.concatenate(stats, axis=0))[:8, :]
-        return [send(rz.at[z], rz.at[z], z_peer[d]) for d in range(1, NZ)]
+        return [send(rz.at[z, pl.ds(0, 4), :], rz.at[z, pl.ds(0, 4), :], z_peer[d]) for d in range(1, NZ)]
 
     def merge_rows(buf, lo, hi):
         tiles = [buf[i] for i in range(lo, hi)]
@@ -225,12 +225,12 @@
     def r2(r_z):
         landed(r_z)
         rx[x] = pack_rows(*merge_rows(rz, 0, NZ))
-        return [send(rx.at[x], rx.at[x], x_peer[d]) for d in range(1, NX)]
+        return [send(rx.at[x, pl.ds(0, 4), :], rx.at[x, pl.ds(0, 4), :], x_peer[d]) for d in range(1, NX)]
 
     def r3(r_x):
         landed(r_x)
         ry[y] = pack_rows(*merge_rows(rx, 0, NX))
-        return [send(ry.at[y], ry.at[y], y_peer[d]) for d in range(1, NY)]
+        return [send(ry.at[y, pl.ds(0, 4), :], ry.at[y, pl.ds(0, 4), :], y_peer[d]) for d in range(1, NY)]
 
     def r4(r_y):
         landed(r_y)

time: 70 us -> 70.1 us (level)
  no operation moved by 1% of the time
where the time goes in v4:
time: 70.1 us; the launch traced here: 69.9 us
  Pallas kernels  69.3 us (99%)
    pallas_call x1, Pallas kernels, per_device(): pl.pallas_call(functools.partial(kernel, v), out_shape=(jax.ShapeDtypeStr...  67.6 us
    pallas_call x1, Pallas kernels, per_device(): pl.pallas_call(hand_over, out_shape=(jax.ShapeDtypeStruct((W,), F32), jax...  1.73 us

profile of v4, /device:TPU:24, one launch (start us, length us, event | category | flops | bytes accessed | tf_op | source)
XLA Modules:
  0.0 69.9 jit_solution(5874500933293505995)
XLA Ops:
  0.6 67.6 %shard_map.86 = (f32[320]{0:T(512)}, bf16[320,512]{1,0:T(8,128)(2,1)}) custom-call(bf16[1,320,1024]{2,1,0:T(8,128)(2,1)} %rh_hbm.1, bf16[1,1187,1024]{2,1,0:T(8,128)(2,1)} %bitcast.2, bf16[320,512]{1,0:T(8,128)(2,1)} %ph_hbm.1, bf16[1187,512]{1,0:T(8,128)(2,1)} %bitcast.3, s32[320]{0:T(512)} %t_hbm.1, s32[320]{0:T(512)} %m_hbm.1, s32[320]{0:T(512)} %i_hbm.1), custom_call_target="tpu_custom_call" | custom-call | tf_op jit(solution)/shard_map/pallas_call | solution.py:447
  68.2 1.7 %shard_map.87 = (f32[320]{0:T(512)}, bf16[320,512]{1,0:T(8,128)(2,1)}) custom-call(f32[320]{0:T(512)} %get-tuple-element.4.rew, bf16[320,512]{1,0:T(8,128)(2,1)} %get-tuple-element.5.hg), custom_call_target="tpu_custom_call" | custom-call | tf_op jit(solution)/shard_map/pallas_call | solution.py:457
